TPU v7x, 128 devices: a whole 4x4x4 slice. The times are simulated.
128 devices in a mesh: src: 8 (over z_lo, x), tgt: 16 (over y, z_hi, core).
Axes of the slice: x: 4, y: 4, z: 4 (z_hi: 2, z_lo: 2; z = z_hi * 2 + z_lo), core: 2. Of those that a mesh axis runs over, the one named last changes fastest.
Arguments:
- src_values: float32 [16, 131072], P(None, ('src', 'tgt')), may hold values from -6 to 6
- src_offset: float32 [131072], P(('src', 'tgt')), may hold values from -1 to 1
- src_box: int32 [131072], P(('src', 'tgt')), may hold values from 0 to 32767, as said below
- tgt_offset: float32 [131072], P(('src', 'tgt')), may hold values from -1 to 1
- tgt_box: int32 [131072], P(('src', 'tgt')), may hold values from 0 to 32767, as said below
- pattern: int32 [15, 32768], P(None, ('src', 'tgt')), may hold values from 0 to 3
- operators: float32 [15, 4, 2, 64, 128], replicated, may hold values from -0.5 to 0.5
Outputs:
- target_values: float32 [16, 131072], P(None, ('src', 'tgt'))
Inputs may be any that keep to these rules, and one draw needn't show every extreme that they name: `src_box`: source point p lies in a box of the block [(p // 1024) * 256, (p // 1024 + 1) * 256). `tgt_box`: target point q lies in a box of the block [(q // 1024) * 256, (q // 1024 + 1) * 256).
All inputs are finite; a program needn't handle non-finite values.
Results may differ from a plain program's by a relative error of at most 0.00016.
Values sent between devices are 32-bit elements; how exact they have to be, the bound alone decides.
A program may use at most 128 MiB of HBM per device.

v0:
```python
import jax
import jax.numpy as jnp
from jax import lax
from jax.sharding import PartitionSpec as P

RANK = 64
KINDS = 4


HIGHEST = lax.Precision.HIGHEST


def partner_2(value, axis, stride):
    return lax.ppermute(value, axis, [(i, i ^ 1 << stride) for i in range(lax.axis_size(axis))])


def chebyshev(points):
    rows = [jnp.ones_like(points), points]
    for order in range(2, RANK):
        rows.append(2.0 * points * rows[-1] - rows[-2])
    return jnp.stack(rows[:RANK])


def reverse_bits(values, nbits):
    lead = values.shape[:-1]
    base = len(lead)
    split = values.reshape(lead + (2,) * nbits)
    order = tuple(range(base)) + tuple(range(base + nbits - 1, base - 1, -1))
    return split.transpose(order).reshape(lead + (2**nbits,))


def local_level(coefficients, weights, pattern_row, bit_pos):
    funcs, count = (coefficients.shape[0], coefficients.shape[2])
    outer = count >> bit_pos + 1
    inner = 1 << bit_pos
    split = coefficients.reshape(funcs, RANK, outer, 2, inner)
    stacked = jnp.concatenate([split[:, :, :, 0, :], split[:, :, :, 1, :]], axis=1)
    matrix = weights.reshape(KINDS * 2 * RANK, 2 * RANK)
    products = jnp.einsum("mr,vrgh->vmgh", matrix, stacked, precision=HIGHEST)
    products = products.reshape(funcs, KINDS, 2, RANK, outer, inner)
    kinds_row = jnp.arange(KINDS)
    selector = (
        pattern_row.reshape(outer, 2, inner)[None] == kinds_row[:, None, None, None]
    ).astype(jnp.float32)
    merged = jnp.einsum("kgch,vkcrgh->vrgch", selector, products, precision=HIGHEST)
    return merged.reshape(funcs, RANK, count)


def remote_level(own, partner, weights, pattern_row, parity):
    first = jnp.where(parity == 0, own, partner)
    second = jnp.where(parity == 0, partner, own)
    stacked = jnp.concatenate([first, second], axis=1)
    chosen = jnp.where(parity == 0, weights[:, 0], weights[:, 1]).reshape(KINDS * RANK, 2 * RANK)
    products = jnp.einsum("mr,vrp->vmp", chosen, stacked, precision=HIGHEST)
    products = products.reshape(own.shape[0], KINDS, RANK, own.shape[2])
    kinds_row = jnp.arange(KINDS, dtype=pattern_row.dtype)
    selector = (pattern_row[None, :] == kinds_row[:, None]).astype(jnp.float32)
    return jnp.einsum("kp,vkrp->vrp", selector, products, precision=HIGHEST)


def on_device(src_values, src_offset, src_box, tgt_offset, tgt_box, pattern, operators):
    funcs = src_values.shape[0]
    boxes_here = pattern.shape[1]
    tgt_bits = lax.axis_size("tgt").bit_length() - 1
    src_bits = lax.axis_size("src").bit_length() - 1
    dev_bits = tgt_bits + src_bits
    devices_count = 1 << dev_bits
    upper_count = boxes_here >> dev_bits
    local_bits = boxes_here.bit_length() - 1
    box_ids = jnp.arange(boxes_here, dtype=jnp.int32)
    basis_src = chebyshev(src_offset)
    src_hot = (jnp.remainder(src_box, boxes_here)[:, None] == box_ids[None, :]).astype(jnp.float32)
    weighted = src_values[:, None, :] * basis_src[None, :, :]
    coefficients = jnp.einsum("vrp,ps->vrs", weighted, src_hot, precision=HIGHEST)
    for level in range(local_bits):
        coefficients = local_level(coefficients, operators[level], pattern[level], level)
    for level in range(dev_bits):
        if level < tgt_bits:
            partner = partner_2(coefficients, "tgt", level)
            parity = lax.axis_index("tgt") >> level & 1
        else:
            partner = partner_2(coefficients, "src", level - tgt_bits)
            parity = lax.axis_index("src") >> level - tgt_bits & 1
        coefficients = remote_level(
            coefficients,
            partner,
            operators[local_bits + level],
            pattern[local_bits + level],
            parity,
        )
    ordered = reverse_bits(coefficients.reshape(funcs, RANK, upper_count, devices_count), dev_bits)
    arrived = lax.all_to_all(ordered, ("src", "tgt"), split_axis=3, concat_axis=3, tiled=True)
    coefficients = arrived.reshape(funcs, RANK, boxes_here)
    final = reverse_bits(coefficients, local_bits)
    final = final.reshape(funcs, RANK, devices_count, upper_count)
    final = jnp.swapaxes(final, 2, 3).reshape(funcs, RANK, boxes_here)
    tgt_hot = (jnp.remainder(tgt_box, boxes_here)[:, None] == box_ids[None, :]).astype(jnp.float32)
    gathered = jnp.einsum("vrs,ps->vrp", final, tgt_hot, precision=HIGHEST)
    basis_tgt = chebyshev(tgt_offset)
    return 0.125 * jnp.einsum("vrp,rp->vp", gathered, basis_tgt, precision=HIGHEST)


def solution(mesh):
    placed = (
        P(None, ("src", "tgt")),
        P(("src", "tgt")),
        P(("src", "tgt")),
        P(("src", "tgt")),
        P(("src", "tgt")),
        P(None, ("src", "tgt")),
        P(),
    )
    return jax.shard_map(
        on_device, mesh=mesh, in_specs=placed, out_specs=P(None, ("src", "tgt")), check_vma=False
    )
```

profile of v0, /device:TPU:1, one launch (start us, length us, event | category | flops | bytes accessed | tf_op | source)
XLA Modules:
  0.0 450.4 jit_solution(4082845308893566551)
XLA Ops:
  0.0 3.9 fusion.105
  4.7 0.9 copy.101
  5.7 0.9 copy.97
  6.7 0.9 copy.93
  7.8 0.9 copy.89
  9.0 2.3 copy.85
  11.6 3.1 copy.81
  15.4 2.3 fusion.12
  17.7 1.3 copy.49
  20.0 5.3 %convolution_bitcast_fusion.7 = f32[16,512,128,1]{1,2,0,3:T(8,128)} fusion(f32[512,128,1]{1,0,2:T(8,128)S(1)} %bitcast.548, f32[16,64,128,1]{1,2,0,3:T(8,128)S(1)} %get-tuple-element.196, f32[16,64,128,1]{1,2,0,3:T(8,128)S(1)} %get-tuple-element.197), kind=kOutput, calls=%fused_computation.31 | convolution fusion | flops 1610874880 | bytes 5505024 | tf_op jit(solution)/shard_map/mr,vrgh->vmgh/dot_general | solution.py:39
  25.2 5.3 %copy.160 = f32[16,512,128,1]{2,1,0,3:T(8,128)} copy(f32[16,512,128,1]{1,2,0,3:T(8,128)} %convolution_bitcast_fusion.7) | data formatting | bytes 8388608
  30.9 2.9 multiply_reduce_fusion.9
  33.7 1.8 copy.78
  37.0 5.1 %convolution_bitcast_fusion.6 = f32[16,512,64,2]{1,2,3,0:T(8,128)} fusion(f32[512,128,1,1]{1,0,3,2:T(8,128)S(1)} %bitcast.547, f32[16,64,64,2]{1,2,3,0:T(8,128)S(1)} %bitcast.528, f32[16,64,64,2]{1,2,3,0:T(8,128)S(1)} %bitcast.531), kind=kOutput, calls=%fused_computation.30 | convolution fusion | flops 1610874880 | bytes 5505024 | tf_op jit(solution)/shard_map/mr,vrgh->vmgh/dot_general | solution.py:39
  42.1 9.9 %reshape.131 = f32[16,4,2,64,64,2]{3,2,1,4,5,0:T(2,128)} reshape(f32[16,512,64,2]{1,2,3,0:T(8,128)} %convolution_bitcast_fusion.6) | data formatting | bytes 8388608 | tf_op jit(solution)/shard_map/reshape | solution.py:40
  52.0 13.1 %fusion.10 = f32[64,2,2,1,16,64]{5,3,4,2,1,0:T(1,128)S(1)} fusion(pred[4,64,2,2,1,1]{0,4,5,3,2,1:T(4,128)(4,1)S(1)} %copy.81, f32[16,4,2,64,64,2]{3,2,1,4,5,0:T(2,128)} %reshape.131), kind=kOutput, calls=%fused_computation.10 | convolution fusion | flops 12582912 | bytes 5243904 | tf_op jit(solution)/shard_map/kgch,vkcrgh->vrgch/dot_general | solution.py:45
  66.6 5.1 %convolution_bitcast_fusion.5 = f32[16,512,32,4]{1,2,3,0:T(8,128)} fusion(f32[512,128,1,1]{1,0,3,2:T(8,128)S(1)} %bitcast.546, f32[16,64,32,4]{1,2,3,0:T(8,128)S(1)} %bitcast.529, f32[16,64,32,4]{1,2,3,0:T(8,128)S(1)} %bitcast.532), kind=kOutput, calls=%fused_computation.29 | convolution fusion | flops 1610874880 | bytes 5505024 | tf_op jit(solution)/shard_map/mr,vrgh->vmgh/dot_general | solution.py:39
  71.7 9.9 %reshape.132 = f32[16,4,2,64,32,4]{3,2,1,4,5,0:T(2,128)} reshape(f32[16,512,32,4]{1,2,3,0:T(8,128)} %convolution_bitcast_fusion.5) | data formatting | bytes 8388608 | tf_op jit(solution)/shard_map/reshape | solution.py:40
  81.6 12.8 %fusion.8 = f32[32,2,4,1,16,64]{5,3,4,2,1,0:T(1,128)S(1)} fusion(pred[4,32,2,4,1,1]{0,4,5,3,2,1:T(4,128)(4,1)S(1)} %copy-done.14, f32[16,4,2,64,32,4]{3,2,1,4,5,0:T(2,128)} %reshape.132), kind=kOutput, calls=%fused_computation.8 | convolution fusion | flops 12582912 | bytes 5243904 | tf_op jit(solution)/shard_map/kgch,vkcrgh->vrgch/dot_general | solution.py:45
  95.4 5.1 %convolution_bitcast_fusion.4 = f32[16,512,16,8]{1,3,2,0:T(8,128)} fusion(f32[512,128,1,1]{1,0,3,2:T(8,128)S(1)} %bitcast.545, f32[16,64,16,8]{1,3,2,0:T(8,128)S(1)} %bitcast.530, f32[16,64,16,8]{1,3,2,0:T(8,128)S(1)} %bitcast.533), kind=kOutput, calls=%fused_computation.28 | convolution fusion | flops 1610874880 | bytes 5505024 | tf_op jit(solution)/shard_map/mr,vrgh->vmgh/dot_general | solution.py:39
  100.5 9.9 %reshape.133 = f32[16,4,2,64,16,8]{3,2,1,5,4,0:T(2,128)} reshape(f32[16,512,16,8]{1,3,2,0:T(8,128)} %convolution_bitcast_fusion.4) | data formatting | bytes 8388608 | tf_op jit(solution)/shard_map/reshape | solution.py:40
  110.4 12.9 %fusion.6 = f32[16,2,8,1,16,64]{5,3,4,2,1,0:T(1,128)S(1)} fusion(pred[4,16,2,8,1,1]{0,4,5,3,2,1:T(4,128)(4,1)S(1)} %copy-done.15, f32[16,4,2,64,16,8]{3,2,1,5,4,0:T(2,128)} %reshape.133), kind=kOutput, calls=%fused_computation.6 | convolution fusion | flops 12582912 | bytes 5243904 | tf_op jit(solution)/shard_map/kgch,vkcrgh->vrgch/dot_general | solution.py:45
  124.3 5.1 %convolution_bitcast_fusion.3 = f32[16,512,8,16]{1,3,2,0:T(8,128)} fusion(f32[512,128,1,1]{1,0,3,2:T(8,128)S(1)} %bitcast.544, f32[16,64,8,16]{1,3,2,0:T(8,128)S(1)} %get-tuple-element.48, f32[16,64,8,16]{1,3,2,0:T(8,128)S(1)} %get-tuple-element.47), kind=kOutput, calls=%fused_computation.27 | convolution fusion | flops 1610874880 | bytes 5505024 | tf_op jit(solution)/shard_map/mr,vrgh->vmgh/dot_general | solution.py:39
  129.4 9.9 %reshape.134 = f32[16,4,2,64,8,16]{3,2,1,5,4,0:T(2,128)} reshape(f32[16,512,8,16]{1,3,2,0:T(8,128)} %convolution_bitcast_fusion.3) | data formatting | bytes 8388608 | tf_op jit(solution)/shard_map/reshape | solution.py:40
  139.3 13.1 %fusion.4 = f32[8,2,16,1,16,64]{5,3,4,2,1,0:T(1,128)S(1)} fusion(pred[4,8,2,16,1,1]{0,4,5,3,2,1:T(4,128)(4,1)S(1)} %copy-done.16, f32[16,4,2,64,8,16]{3,2,1,5,4,0:T(2,128)} %reshape.134), kind=kOutput, calls=%fused_computation.4 | convolution fusion | flops 12582912 | bytes 5243904 | tf_op jit(solution)/shard_map/kgch,vkcrgh->vrgch/dot_general | solution.py:45
  153.3 5.1 %convolution_bitcast_fusion.2 = f32[16,512,4,32]{1,3,2,0:T(8,128)} fusion(f32[512,128,1,1]{1,0,3,2:T(8,128)S(1)} %bitcast.543, f32[16,64,4,32]{1,3,2,0:T(8,128)S(1)} %get-tuple-element.46, f32[16,64,4,32]{1,3,2,0:T(8,128)S(1)} %get-tuple-element.45), kind=kOutput, calls=%fused_computation.26 | convolution fusion | flops 1610874880 | bytes 5505024 | tf_op jit(solution)/shard_map/mr,vrgh->vmgh/dot_general | solution.py:39
  158.5 9.9 %reshape.135 = f32[16,4,2,64,4,32]{3,2,1,5,4,0:T(2,128)} reshape(f32[16,512,4,32]{1,3,2,0:T(8,128)} %convolution_bitcast_fusion.2) | data formatting | bytes 8388608 | tf_op jit(solution)/shard_map/reshape | solution.py:40
  168.4 12.8 %fusion.2 = f32[4,2,32,1,16,64]{5,3,4,2,1,0:T(1,128)S(1)} fusion(pred[4,4,2,32,1,1]{0,4,5,3,2,1:T(4,128)(4,1)S(1)} %copy-done.18, f32[16,4,2,64,4,32]{3,2,1,5,4,0:T(2,128)} %reshape.135), kind=kOutput, calls=%fused_computation.2 | convolution fusion | flops 12582912 | bytes 5243904 | tf_op jit(solution)/shard_map/kgch,vkcrgh->vrgch/dot_general | solution.py:45
  182.2 5.1 %convolution_bitcast_fusion.1 = f32[16,512,2,64]{1,3,2,0:T(8,128)} fusion(f32[512,128,1,1]{1,0,3,2:T(8,128)S(1)} %bitcast.542, f32[16,64,2,64]{1,3,2,0:T(8,128)S(1)} %get-tuple-element.44, f32[16,64,2,64]{1,3,2,0:T(8,128)S(1)} %get-tuple-element.43), kind=kOutput, calls=%fused_computation.25 | convolution fusion | flops 1610874880 | bytes 5505024 | tf_op jit(solution)/shard_map/mr,vrgh->vmgh/dot_general | solution.py:39
  187.2 9.9 %reshape.136 = f32[16,4,2,64,2,64]{3,2,1,5,4,0:T(2,128)} reshape(f32[16,512,2,64]{1,3,2,0:T(8,128)} %convolution_bitcast_fusion.1) | data formatting | bytes 8388608 | tf_op jit(solution)/shard_map/reshape | solution.py:40
  197.2 12.9 %fusion = f32[2,2,64,1,16,64]{5,3,4,2,1,0:T(1,128)S(1)} fusion(pred[4,2,2,64,1,1]{0,4,5,3,2,1:T(4,128)(4,1)S(1)} %copy-done.17, f32[16,4,2,64,2,64]{3,2,1,5,4,0:T(2,128)} %reshape.136), kind=kOutput, calls=%fused_computation | convolution fusion | flops 12582912 | bytes 5243904 | tf_op jit(solution)/shard_map/kgch,vkcrgh->vrgch/dot_general | solution.py:45
  210.9 5.0 %convolution_bitcast_fusion = f32[16,512,1,128]{1,3,0,2:T(8,128)} fusion(f32[512,128,1]{1,0,2:T(8,128)S(1)} %bitcast.541, f32[16,64,1,128]{1,3,0,2:T(8,128)S(1)} %get-tuple-element.42, f32[16,64,1,128]{1,3,0,2:T(8,128)S(1)} %get-tuple-element.41), kind=kOutput, calls=%fused_computation.24 | convolution fusion | flops 1610874880 | bytes 5505024 | tf_op jit(solution)/shard_map/mr,vrgh->vmgh/dot_general | solution.py:39
  216.0 5.3 %copy.161 = f32[16,512,1,128]{3,1,0,2:T(8,128)} copy(f32[16,512,1,128]{1,3,0,2:T(8,128)} %convolution_bitcast_fusion) | data formatting | bytes 8388608
  221.4 2.9 multiply_reduce_fusion.8
  225.1 0.8 reshape.139
  225.9 1.9 collective-permute-start
  227.8 2.2 collective-permute-done
  230.3 3.6 fusion.14
  234.5 3.8 collective-permute-start.1
  238.3 23.2 %collective-permute-done.1 = f32[16,64,256]{2,1,0:T(8,128)S(1)} collective-permute-done((f32[16,64,256]{2,1,0:T(8,128)S(1)}, f32[16,64,256]{2,1,0:T(8,128)S(1)}, u32[]{:S(2)}, u32[]{:S(2)}) %collective-permute-start.1) | collective-permute-done | bytes 1048608 | tf_op jit(solution)/shard_map/ppermute | solution.py:14
  261.7 3.6 fusion.18
  265.9 1.5 collective-permute-start.2
  267.5 22.4 %collective-permute-done.2 = f32[16,64,256]{2,1,0:T(8,128)S(1)} collective-permute-done((f32[16,64,256]{2,1,0:T(8,128)S(1)}, f32[16,64,256]{2,1,0:T(8,128)S(1)}, u32[]{:S(2)}, u32[]{:S(2)}) %collective-permute-start.2) | collective-permute-done | bytes 1048608 | tf_op jit(solution)/shard_map/ppermute | solution.py:14
  290.2 3.6 fusion.22
  294.3 3.0 collective-permute-start.3
  297.4 21.4 %collective-permute-done.3 = f32[16,64,256]{2,1,0:T(8,128)S(1)} collective-permute-done((f32[16,64,256]{2,1,0:T(8,128)S(1)}, f32[16,64,256]{2,1,0:T(8,128)S(1)}, u32[]{:S(2)}, u32[]{:S(2)}) %collective-permute-start.3) | collective-permute-done | bytes 1048608 | tf_op jit(solution)/shard_map/ppermute | solution.py:14
  319.0 3.6 fusion.26
  323.2 1.5 collective-permute-start.4
  324.8 20.7 %collective-permute-done.4 = f32[16,64,256]{2,1,0:T(8,128)S(1)} collective-permute-done((f32[16,64,256]{2,1,0:T(8,128)S(1)}, f32[16,64,256]{2,1,0:T(8,128)S(1)}, u32[]{:S(2)}, u32[]{:S(2)}) %collective-permute-start.4) | collective-permute-done | bytes 1048608 | tf_op jit(solution)/shard_map/ppermute | solution.py:14
  345.6 3.6 fusion.30
  349.8 2.9 collective-permute-start.5
  352.7 19.7 %collective-permute-done.5 = f32[16,64,256]{2,1,0:T(8,128)S(1)} collective-permute-done((f32[16,64,256]{2,1,0:T(8,128)S(1)}, f32[16,64,256]{2,1,0:T(8,128)S(1)}, u32[]{:S(2)}, u32[]{:S(2)}) %collective-permute-start.5) | collective-permute-done | bytes 1048608 | tf_op jit(solution)/shard_map/ppermute | solution.py:14
  372.6 3.6 fusion.34
  377.2 20.0 %collective-permute-done.6 = f32[16,64,256]{2,1,0:T(8,128)S(1)} collective-permute-done((f32[16,64,256]{2,1,0:T(8,128)S(1)}, f32[16,64,256]{2,1,0:T(8,128)S(1)}, u32[]{:S(2)}, u32[]{:S(2)}) %collective-permute-start.6) | collective-permute-done | bytes 1048608 | tf_op jit(solution)/shard_map/ppermute | solution.py:14
  397.5 3.6 fusion.38
  401.6 1.3 copy.153
  403.4 2.3 reshape.235
  405.7 13.6 %all-to-all-start = ((f32[128,1,2048]{2,1,0:T(1,128)}), f32[128,1,2048]{2,1,0:T(1,128)S(1)}, u32[]{:S(2)}, u32[]{:S(2)}) async-start(f32[128,1,2048]{2,1,0:T(1,128)} %reshape.235), calls=%async_computation | async-start | bytes 2097152 | tf_op jit(solution)/shard_map/all_to_all | solution.py:92
  420.0 18.1 %all-to-all-done = f32[128,1,2048]{2,1,0:T(1,128)S(1)} async-done(((f32[128,1,2048]{2,1,0:T(1,128)}), f32[128,1,2048]{2,1,0:T(1,128)S(1)}, u32[]{:S(2)}, u32[]{:S(2)}) %all-to-all-start) | async-done | bytes 1048608 | tf_op jit(solution)/shard_map/all_to_all | solution.py:92
  438.6 3.1 reduce.48
  442.6 1.6 copy.69
  444.2 2.1 copy.70
  446.3 0.8 reshape.148
  447.2 2.1 multiply_reduce_fusion
  (140 shorter events, 20.6 us)
Async XLA Ops:
  0.0 4.0 copy-start.21
  0.0 14.7 %copy-start.19 = (f32[1024]{0:T(1024)S(1)}, f32[1024]{0:T(1024)}, u32[]{:S(2)}) copy-start(f32[1024]{0:T(1024)} %param.8) | copy-start | bytes 12292
  0.0 14.9 %copy-start.28 = (s32[1024]{0:T(1024)S(1)}, s32[1024]{0:T(1024)}, u32[]{:S(2)}) copy-start(s32[1024]{0:T(1024)} %param.9) | copy-start | bytes 12292
  0.0 15.4 %copy-start.30 = (f32[16,1024]{1,0:T(8,128)S(1)}, f32[16,1024]{1,0:T(8,128)}, u32[]{:S(2)}) copy-start(f32[16,1024]{1,0:T(8,128)} %param.7) | copy-start | bytes 196612
  19.0 1.0 copy-start.6
  35.6 1.4 copy-start.5
  65.1 1.5 copy-start.4
  71.7 9.9 %copy-start.14 = (pred[4,32,2,4,1,1]{0,4,5,3,2,1:T(4,128)(4,1)S(1)}, pred[4,32,2,4,1,1]{0,4,5,3,2,1:T(4,128)(4,1)}, u32[]{:S(2)}) copy-start(pred[4,32,2,4,1,1]{0,4,5,3,2,1:T(4,128)(4,1)} %copy.85) | copy-start | bytes 3076
  94.5 1.0 copy-start.3
  100.5 9.9 %copy-start.15 = (pred[4,16,2,8,1,1]{0,4,5,3,2,1:T(4,128)(4,1)S(1)}, pred[4,16,2,8,1,1]{0,4,5,3,2,1:T(4,128)(4,1)}, u32[]{:S(2)}) copy-start(pred[4,16,2,8,1,1]{0,4,5,3,2,1:T(4,128)(4,1)} %copy.89) | copy-start | bytes 3076
  123.3 1.0 copy-start.2
  129.4 9.9 %copy-start.16 = (pred[4,8,2,16,1,1]{0,4,5,3,2,1:T(4,128)(4,1)S(1)}, pred[4,8,2,16,1,1]{0,4,5,3,2,1:T(4,128)(4,1)}, u32[]{:S(2)}) copy-start(pred[4,8,2,16,1,1]{0,4,5,3,2,1:T(4,128)(4,1)} %copy.93) | copy-start | bytes 3076
  152.4 1.0 copy-start.1
  158.5 9.9 %copy-start.18 = (pred[4,4,2,32,1,1]{0,4,5,3,2,1:T(4,128)(4,1)S(1)}, pred[4,4,2,32,1,1]{0,4,5,3,2,1:T(4,128)(4,1)}, u32[]{:S(2)}) copy-start(pred[4,4,2,32,1,1]{0,4,5,3,2,1:T(4,128)(4,1)} %copy.97) | copy-start | bytes 3076
  181.2 1.0 copy-start
  187.2 9.9 %copy-start.17 = (pred[4,2,2,64,1,1]{0,4,5,3,2,1:T(4,128)(4,1)S(1)}, pred[4,2,2,64,1,1]{0,4,5,3,2,1:T(4,128)(4,1)}, u32[]{:S(2)}) copy-start(pred[4,2,2,64,1,1]{0,4,5,3,2,1:T(4,128)(4,1)} %copy.101) | copy-start | bytes 3076
  216.0 5.3 %copy-start.27 = (s32[1,256]{1,0:T(1,128)S(1)}, s32[1,256]{1,0:T(1,128)}, u32[]{:S(2)}) copy-start(s32[1,256]{1,0:T(1,128)} %get-tuple-element.63) | copy-start | bytes 3076
  221.3 6.5 %copy-start.26 = (s32[1,256]{1,0:T(1,128)S(1)}, s32[1,256]{1,0:T(1,128)}, u32[]{:S(2)}) copy-start(s32[1,256]{1,0:T(1,128)} %get-tuple-element.62) | copy-start | bytes 3076
  221.3 6.5 %copy-start.13 = (f32[4,2,64,128]{3,2,1,0:T(8,128)S(1)}, f32[4,2,64,128]{3,2,1,0:T(8,128)}, u32[]{:S(2)}) copy-start(f32[4,2,64,128]{3,2,1,0:T(8,128)} %get-tuple-element.17) | copy-start | bytes 786436
  225.9 4.2 collective-permute-start
  234.0 4.3 copy-start.25
  234.0 4.3 copy-start.12
  234.5 27.0 %collective-permute-start.1 = (f32[16,64,256]{2,1,0:T(8,128)S(1)}, f32[16,64,256]{2,1,0:T(8,128)S(1)}, u32[]{:S(2)}, u32[]{:S(2)}) collective-permute-start(f32[16,64,256]{2,1,0:T(8,128)S(1)} %bitcast.537), channel_id=1, source_target_pairs={{0,2},{1,3},{2,0},{3,1},{4,6},{5,7},{6,4},{7,5},{8,10},{9,11},{10,... | collective-permute-start | bytes 3145736 | tf_op jit(solution)/shard_map/ppermute | solution.py:14
  265.4 2.1 copy-start.24
  265.4 2.1 copy-start.11
  265.9 24.0 %collective-permute-start.2 = (f32[16,64,256]{2,1,0:T(8,128)S(1)}, f32[16,64,256]{2,1,0:T(8,128)S(1)}, u32[]{:S(2)}, u32[]{:S(2)}) collective-permute-start(f32[16,64,256]{2,1,0:T(8,128)S(1)} %bitcast.538), channel_id=1, source_target_pairs={{0,4},{1,5},{2,6},{3,7},{4,0},{5,1},{6,2},{7,3},{8,12},{9,13},{10,... | collective-permute-start | bytes 3145736 | tf_op jit(solution)/shard_map/ppermute | solution.py:14
  293.8 3.5 copy-start.23
  293.8 3.5 copy-start.10
  294.3 24.4 %collective-permute-start.3 = (f32[16,64,256]{2,1,0:T(8,128)S(1)}, f32[16,64,256]{2,1,0:T(8,128)S(1)}, u32[]{:S(2)}, u32[]{:S(2)}) collective-permute-start(f32[16,64,256]{2,1,0:T(8,128)S(1)} %bitcast.536), channel_id=1, source_target_pairs={{0,8},{1,9},{2,10},{3,11},{4,12},{5,13},{6,14},{7,15},{8,0},{9,1},... | collective-permute-start | bytes 3145736 | tf_op jit(solution)/shard_map/ppermute | solution.py:14
  322.6 2.1 copy-start.22
  322.7 2.1 copy-start.9
  323.2 22.2 %collective-permute-start.4 = (f32[16,64,256]{2,1,0:T(8,128)S(1)}, f32[16,64,256]{2,1,0:T(8,128)S(1)}, u32[]{:S(2)}, u32[]{:S(2)}) collective-permute-start(f32[16,64,256]{2,1,0:T(8,128)S(1)} %bitcast.534), channel_id=1, source_target_pairs={{0,16},{16,0},{32,48},{48,32},{64,80},{80,64},{96,112},{112,96},{1... | collective-permute-start | bytes 3145736 | tf_op jit(solution)/shard_map/ppermute | solution.py:14
  349.3 3.4 copy-start.8
  349.8 22.6 %collective-permute-start.5 = (f32[16,64,256]{2,1,0:T(8,128)S(1)}, f32[16,64,256]{2,1,0:T(8,128)S(1)}, u32[]{:S(2)}, u32[]{:S(2)}) collective-permute-start(f32[16,64,256]{2,1,0:T(8,128)S(1)} %bitcast.539), channel_id=1, source_target_pairs={{0,32},{16,48},{32,0},{48,16},{64,96},{80,112},{96,64},{112,80},{1... | collective-permute-start | bytes 3145736 | tf_op jit(solution)/shard_map/ppermute | solution.py:14
  376.3 1.0 copy-start.7
  376.8 20.4 %collective-permute-start.6 = (f32[16,64,256]{2,1,0:T(8,128)S(1)}, f32[16,64,256]{2,1,0:T(8,128)S(1)}, u32[]{:S(2)}, u32[]{:S(2)}) collective-permute-start(f32[16,64,256]{2,1,0:T(8,128)S(1)} %bitcast.535), channel_id=1, source_target_pairs={{0,64},{16,80},{32,96},{48,112},{64,0},{80,16},{96,32},{112,48},{1... | collective-permute-start | bytes 3145736 | tf_op jit(solution)/shard_map/ppermute | solution.py:14
  403.2 16.1 %copy-start.20 = (f32[1024]{0:T(1024)S(1)}, f32[1024]{0:T(1024)}, u32[]{:S(2)}) copy-start(f32[1024]{0:T(1024)} %param.10) | copy-start | bytes 12292
  403.2 16.8 %copy-start.29 = (s32[1024]{0:T(1024)S(1)}, s32[1024]{0:T(1024)}, u32[]{:S(2)}) copy-start(s32[1024]{0:T(1024)} %param.11) | copy-start | bytes 12292
  405.7 32.4 %all-to-all-start = ((f32[128,1,2048]{2,1,0:T(1,128)}), f32[128,1,2048]{2,1,0:T(1,128)S(1)}, u32[]{:S(2)}, u32[]{:S(2)}) async-start(f32[128,1,2048]{2,1,0:T(1,128)} %reshape.235), calls=%async_computation | async-start | bytes 2097152 | tf_op jit(solution)/shard_map/all_to_all | solution.py:92
where the time goes:
time: 458 us; the launch traced here: 450 us
  matrix products  148 us (32%)
  waiting for transfers between devices  148 us (32%)
  local copies, waits for them, and re-layouts  109 us (24%)
  starting transfers between devices  28.5 us (6%)
  other arithmetic  15.5 us (3%)
    ppermute x7, waiting for transfers between devices, partner_2(): lax.ppermute(value, axis, [(i, i ^ 1 << stride) for i in range(lax.axis_s...  130 us
    dot_general x6, matrix products, local_level(): jnp.einsum('kgch,vkcrgh->vrgch', selector, products, precision=HIGHEST)  77.6 us
    reshape x6, local copies, waits for them, and re-layouts, local_level(): products = products.reshape(funcs, KINDS, 2, RANK, outer, inner)  59.4 us
    dot_general x8, matrix products, local_level(): products = jnp.einsum('mr,vrgh->vmgh', matrix, stacked, precision=HIGHEST)  41 us
    dot_general x7, matrix products, remote_level(): products = jnp.einsum('mr,vrp->vmp', chosen, stacked, precision=HIGHEST)  25.4 us
    all_to_all x1, waiting for transfers between devices, on_device(): lax.all_to_all(ordered, ('src', 'tgt'), split_axis=3, concat_axis=3, tile...  18.1 us
    unnamed x73, local copies, waits for them, and re-layouts  17.4 us
    ppermute x7, starting transfers between devices, partner_2(): lax.ppermute(value, axis, [(i, i ^ 1 << stride) for i in range(lax.axis_s...  15 us
  transfers between devices with their start and end apart: 8, of which 8 were waited for; matrix products, arithmetic and copies ran while one was open for 0% of the time, Pallas kernels for 0%

commit v1 on v0

v1 whole, which is shorter than its diff:
```python
import functools

import jax
import jax.numpy as jnp
from jax import lax
from jax.experimental import pallas as pl
from jax.experimental.pallas import tpu as pltpu
from jax.sharding import PartitionSpec as P

RANK = 64
KINDS = 4
LANES = 2 * RANK
MESH = pl.DeviceIdType.MESH
F32, BF16 = jnp.float32, jnp.bfloat16
NT = (((1,), (1,)), ((), ()))
NN = (((1,), (0,)), ((), ()))


def split(x):
    hi = x.astype(BF16)
    return hi, (x - hi.astype(F32)).astype(BF16)


def dot(a, b, dims):
    return lax.dot_general(a, b, dims, preferred_element_type=F32)


def bit(x, k):
    return (x >> k) & 1


def reverse7(x):
    return sum(bit(x, k) << (6 - k) for k in range(7))


def reverse7_scalar(x):
    return sum(((x // 2**k) % 2) * 2 ** (6 - k) for k in range(7))


def row_of(box, level):
    parts = [bit(box, level - 1 - k) << k for k in range(level)]
    parts += [bit(box, 7 + level - k) << k for k in range(level, 7)]
    return sum(parts)


def chebyshev(points):
    n = points.shape[1]
    x = jnp.broadcast_to(points, (8, n))
    rows = [jnp.ones_like(x), x]
    for _ in range(7):
        rows.append(2.0 * x * rows[-1] - rows[-2])
    at = lax.broadcasted_iota(jnp.int32, (8, n), 0)
    now, before = rows[0], rows[8]
    for k in range(1, 8):
        now = jnp.where(at == k, rows[k], now)
        before = jnp.where(at == k, rows[8 - k], before)
    twice = 2.0 * rows[8]
    blocks = [now]
    for _ in range(RANK // 8 - 1):
        now, before = twice * now - before, now
        blocks.append(now)
    return jnp.concatenate(blocks, axis=0)


def half_masks(basis, child):
    return jnp.concatenate([jnp.where(child == c, basis, 0.0) for c in range(2)], axis=0)


def kernel(
    funcs_part, parts, tgt_size, devices,
    values_ref, src_offset_ref, src_box_ref, tgt_offset_ref, tgt_box_ref, pattern_ref, weights_ref,
    out_ref,
    work, wide, kinds, basis_in, basis_out, sent, arrived, pattern_sent, pattern_arrived,
    send_sem, recv_sem, pattern_send_sem, pattern_recv_sem,
):
    V = funcs_part
    src_me, tgt_me = lax.axis_index("src"), lax.axis_index("tgt")
    me = src_me * tgt_size + tgt_me
    slot = reverse7_scalar(me)

    def peer(k):
        other = (me + k) % devices
        return other, (other // tgt_size, other % tgt_size)

    barrier = pltpu.get_barrier_semaphore()

    @pl.loop(1, devices)
    def _(k):
        pl.semaphore_signal(barrier, inc=1, device_id=peer(k)[1], device_id_type=MESH)

    lane_low = lax.broadcasted_iota(jnp.int32, (1, 1, LANES), 2) < RANK

    def set_kinds(index, level, values, order, order_rows):
        rows = lax.broadcasted_iota(jnp.int32, (128, 256), 0)
        picked = jnp.where(row_of(order, level) == rows, values, 0.0).astype(BF16)
        lane_child = (lax.broadcasted_iota(jnp.int32, (256, LANES), 1) >= RANK).astype(jnp.int32)
        spread = jnp.where(bit(order_rows, level) == lane_child, 1.0, 0.0).astype(BF16)
        kinds[index] = dot(picked, spread, NN)

    def exchange_store(y, ref):
        y = y.reshape(128, V, LANES)
        top, low = y[:64], y[64:]
        n0 = jnp.where(lane_low, top, pltpu.roll(low.reshape(64 * V, LANES), RANK, 1).reshape(64, V, LANES))
        n1 = jnp.where(lane_low, pltpu.roll(top.reshape(64 * V, LANES), RANK, 1).reshape(64, V, LANES), low)
        ref[...] = jnp.stack([n0, n1], axis=1).reshape(128 * V, LANES)

    def level_product(index, x):
        hi, lo = split(weights_ref[index])
        wide[:, :LANES] = hi
        wide[:, LANES : 2 * LANES] = hi
        wide[:, 2 * LANES :] = lo
        hi, lo = split(x)
        product = dot(jnp.concatenate([hi, lo, hi], axis=1), wide[...], NT).reshape(128, V, KINDS * LANES)
        kind = jnp.concatenate(
            [jnp.broadcast_to(kinds[index, pl.ds(g, 1), :], (V, LANES))[None] for g in range(128)], axis=0
        )
        y = product[:, :, :LANES]
        for k in range(1, KINDS):
            y = jnp.where(kind == float(k), product[:, :, k * LANES : (k + 1) * LANES], y)
        return y

    def inner_levels(first):
        @pl.loop(0, 6)
        def _(i):
            now = lax.rem(i, 2)
            exchange_store(level_product(first + i, work[now]), work.at[1 - now])

    order = lax.broadcasted_iota(jnp.int32, (1, 256), 1)
    order_rows = lax.broadcasted_iota(jnp.int32, (256, LANES), 0)
    for level in range(7):
        set_kinds(level, level, pattern_ref[level : level + 1, :].astype(F32), order, order_rows)
    rows = []
    for level in range(7, 15):
        row = pattern_ref[level : level + 1, :].astype(F32)
        rows += [row[:, :128], row[:, 128:]]
    rows = jnp.concatenate(rows + [jnp.zeros((128 - len(rows), 128), F32)], axis=0).astype(BF16)
    to_device = lax.broadcasted_iota(jnp.int32, (128, 128), 0)
    from_box = lax.broadcasted_iota(jnp.int32, (128, 128), 1)
    permute = jnp.where(reverse7(to_device) == from_box, 1.0, 0.0).astype(BF16)
    pattern_sent[...] = dot(permute, rows, NT)[:, None, :]

    src_box = src_box_ref[...]
    src_row = reverse7((src_box >> 1) & 127)
    hi, lo = split(half_masks(chebyshev(src_offset_ref[...]), src_box & 1))
    basis_in[:LANES] = hi
    basis_in[LANES:] = lo
    tgt_box = tgt_box_ref[...]
    tgt_row = (tgt_box >> 1) & 127
    hi, lo = split(half_masks(chebyshev(tgt_offset_ref[...]), tgt_box & 1))
    basis_out[:LANES] = hi
    basis_out[LANES : 2 * LANES] = hi
    basis_out[2 * LANES :] = lo

    def expand(part, ref):
        values = values_ref[part * V : (part + 1) * V, :]
        hi, lo = split(values)
        hi, lo = hi.astype(F32)[None], lo.astype(F32)[None]
        B = 64

        @pl.loop(0, 128 // B)
        def _(b):
            g = lax.broadcasted_iota(jnp.int32, (B, 1, 1), 0) + b * B
            here = src_row[None] == g
            a = jnp.where(here, hi, 0.0).reshape(B * V, -1).astype(BF16)
            total = dot(a, basis_in[...], NT)
            a = jnp.where(here, lo, 0.0).reshape(B * V, -1).astype(BF16)
            total += dot(a, basis_in[...], NT)
            ref[pl.ds(pl.multiple_of(b * B * V, 8), B * V), :] = total[:, :LANES] + total[:, LANES:]

    def evaluate(part, x):
        hi, lo = split(x)
        x = jnp.concatenate([hi, lo, hi], axis=1)
        n = tgt_row.shape[1]
        Q = 256
        for q in range(0, n, Q):
            h = dot(x, basis_out[:, q : q + Q], NN).reshape(128, V, Q)
            g = lax.broadcasted_iota(jnp.int32, (128, 1, 1), 0)
            total = jnp.sum(jnp.where(tgt_row[None, :, q : q + Q] == g, h, 0.0), axis=0)
            out_ref[part * V : (part + 1) * V, q : q + Q] = 0.125 * total

    def up(part):
        expand(part, work.at[0])
        inner_levels(0)
        exchange_store(level_product(6, work[0]), sent.at[part])

    def block_copy(part, k):
        other, device = peer(k)
        return pltpu.make_async_remote_copy(
            src_ref=sent.at[part, pl.ds(pl.multiple_of(other * V, 8), V)],
            dst_ref=arrived.at[part, pl.ds(pl.multiple_of(slot * V, 8), V)],
            send_sem=send_sem.at[part],
            recv_sem=recv_sem.at[part],
            device_id=device,
            device_id_type=MESH,
        )

    def pattern_copy(k):
        other, device = peer(k)
        return pltpu.make_async_remote_copy(
            src_ref=pattern_sent.at[other],
            dst_ref=pattern_arrived.at[me],
            send_sem=pattern_send_sem,
            recv_sem=pattern_recv_sem,
            device_id=device,
            device_id_type=MESH,
        )

    def send(part):
        @pl.loop(1, devices)
        def _(k):
            block_copy(part, k).start()

        arrived[part, pl.ds(pl.multiple_of(slot * V, 8), V)] = sent[part, pl.ds(pl.multiple_of(me * V, 8), V)]

    def wait_all(ref, sem):
        pltpu.make_async_copy(ref, ref, sem).wait()

    others = pl.ds(0, (devices - 1) * V)

    up(0)
    pl.semaphore_wait(barrier, devices - 1)

    @pl.loop(1, devices)
    def _(k):
        pattern_copy(k).start()

    pattern_arrived[me] = pattern_sent[me]
    send(0)
    for part in range(1, parts):
        up(part)
        send(part)

    wait_all(pattern_arrived.at[pl.ds(0, devices - 1)], pattern_recv_sem)
    got = pattern_arrived[:, 0, :].astype(BF16)
    pick = jnp.where(to_device == from_box, 1.0, 0.0).astype(BF16)
    got = dot(pick, got, NT)
    lanes = lax.broadcasted_iota(jnp.int32, (1, 256), 1)
    order = ((lanes & 127) << 1) + (lanes >> 7)
    order_rows = ((order_rows & 127) << 1) + (order_rows >> 7)
    for level in range(8):
        row = jnp.concatenate([got[2 * level : 2 * level + 1], got[2 * level + 1 : 2 * level + 2]], axis=1)
        set_kinds(7 + level, level, row, order, order_rows)

    for part in range(parts):
        wait_all(arrived.at[part, others], recv_sem.at[part])
        exchange_store(level_product(7, arrived[part]), work.at[0])
        inner_levels(8)
        evaluate(part, level_product(14, work[0]).reshape(128 * V, LANES))

    wait_all(pattern_sent.at[pl.ds(0, devices - 1)], pattern_send_sem)
    for part in range(parts):
        wait_all(sent.at[part, others], send_sem.at[part])


def solution(mesh):
    src_size, tgt_size = mesh.shape["src"], mesh.shape["tgt"]
    devices = src_size * tgt_size
    parts = 2

    def on_device(src_values, src_offset, src_box, tgt_offset, tgt_box, pattern, operators):
        funcs, points = src_values.shape
        V = funcs // parts
        rows = 128 * V
        vmem = pl.BlockSpec(memory_space=pltpu.VMEM)
        return pl.pallas_call(
            functools.partial(kernel, V, parts, tgt_size, devices),
            out_shape=jax.ShapeDtypeStruct((funcs, points), F32),
            in_specs=[vmem] * 7,
            out_specs=vmem,
            scratch_shapes=[
                pltpu.VMEM((2, rows, LANES), F32),
                pltpu.VMEM((KINDS * LANES, 3 * LANES), BF16),
                pltpu.VMEM((15, 128, LANES), F32),
                pltpu.VMEM((2 * LANES, points), BF16),
                pltpu.VMEM((3 * LANES, points), BF16),
                pltpu.VMEM((parts, rows, LANES), F32),
                pltpu.VMEM((parts, rows, LANES), F32),
                pltpu.VMEM((devices, 1, LANES), F32),
                pltpu.VMEM((devices, 1, LANES), F32),
                pltpu.SemaphoreType.DMA((parts,)),
                pltpu.SemaphoreType.DMA((parts,)),
                pltpu.SemaphoreType.DMA,
                pltpu.SemaphoreType.DMA,
            ],
            compiler_params=pltpu.CompilerParams(
                collective_id=0, has_side_effects=True, vmem_limit_bytes=56 * 2**20
            ),
        )(
            src_values,
            src_offset.reshape(1, points),
            src_box.reshape(1, points) & 255,
            tgt_offset.reshape(1, points),
            tgt_box.reshape(1, points) & 255,
            pattern,
            operators.reshape(15, KINDS * LANES, LANES),
        )

    placed = (
        P(None, ("src", "tgt")),
        P(("src", "tgt")),
        P(("src", "tgt")),
        P(("src", "tgt")),
        P(("src", "tgt")),
        P(None, ("src", "tgt")),
        P(),
    )
    return jax.shard_map(
        on_device, mesh=mesh, in_specs=placed, out_specs=P(None, ("src", "tgt")), check_vma=False
    )
```

time: 458 us -> 54.5 us (0.12); the launches traced: 450 us -> 54.2 us
  matrix products: 148 us -> 0 us
  waiting for transfers between devices: 148 us -> 0 us
  local copies, waits for them, and re-layouts: 109 us -> 1.47 us
  Pallas kernels: 0 us -> 50.2 us
  starting transfers between devices: 28.5 us -> 0 us
  other arithmetic: 15.5 us -> 2.56 us
    dot_general x23 -> x0, matrix products: 148 us -> none  [the longest x6 77.6 us: local_level(): jnp.einsum('kgch,vkcrgh->vrgch', selector, products, precision=HIGHEST)]
    ppermute x7 -> x0, waiting for transfers between devices: 130 us -> none  [partner_2(): lax.ppermute(value, axis, [(i, i ^ 1 << stride) for i in range(lax.axis_s...]
    reshape x9 -> x0, local copies, waits for them, and re-layouts: 61.3 us -> none  [the longest x6 59.4 us: local_level(): products = products.reshape(funcs, KINDS, 2, RANK, outer, inner)]
    pallas_call x0 -> x1, Pallas kernels: none -> 50.2 us  [on_device(): pl.pallas_call(functools.partial(kernel, V, parts, tgt_size, devices), ou...]
    all_to_all x1 -> x0, waiting for transfers between devices: 18.1 us -> none  [on_device(): lax.all_to_all(ordered, ('src', 'tgt'), split_axis=3, concat_axis=3, tile...]
    unnamed x73 -> x1, local copies, waits for them, and re-layouts: 17.4 us -> 1.47 us
    ppermute x7 -> x0, starting transfers between devices: 15 us -> none  [partner_2(): lax.ppermute(value, axis, [(i, i ^ 1 << stride) for i in range(lax.axis_s...]
    all_to_all x1 -> x0, starting transfers between devices: 13.6 us -> none  [on_device(): lax.all_to_all(ordered, ('src', 'tgt'), split_axis=3, concat_axis=3, tile...]
  transfers between devices with their start and end apart: 8 -> 0, of which waited for: 8 -> 0; matrix products, arithmetic and copies ran while one was open for 0% -> 0% of each run, Pallas kernels for 0% -> 0%
where the time goes in v1:
time: 54.5 us; the launch traced here: 54.2 us
  Pallas kernels  50.2 us (92%)
  other arithmetic  2.56 us (5%)
  local copies, waits for them, and re-layouts  1.47 us (3%)
    pallas_call x1, Pallas kernels, on_device(): pl.pallas_call(functools.partial(kernel, V, parts, tgt_size, devices), ou...  50.2 us
    unnamed x1, local copies, waits for them, and re-layouts  1.47 us
    and x1, other arithmetic, on_device(): src_box.reshape(1, points) & 255  1.28 us
    and x1, other arithmetic, on_device(): tgt_box.reshape(1, points) & 255  1.28 us

profile of v1, /device:TPU:1, one launch (start us, length us, event | category | flops | bytes accessed | tf_op | source)
XLA Modules:
  0.0 54.2 jit_solution(3718283956720454351)
XLA Ops:
  0.0 1.3 %broadcast_and_fusion.1 = s32[1024]{0:T(1024)} fusion(s32[1024]{0:T(1024)} %param.9), kind=kLoop, calls=%fused_computation.1 | loop fusion | flops 1024 | bytes 8192 | tf_op jit(solution)/shard_map/and | solution.py:291
  1.3 1.3 %broadcast_and_fusion = s32[1024]{0:T(1024)} fusion(s32[1024]{0:T(1024)} %param.11), kind=kLoop, calls=%fused_computation | loop fusion | flops 1024 | bytes 8192 | tf_op jit(solution)/shard_map/and | solution.py:293
  2.6 50.2 %shard_map.73 = f32[16,1024]{1,0:T(8,128)} custom-call(f32[16,1024]{1,0:T(8,128)} %values_ref.1, f32[1,1024]{1,0:T(1,128)} %bitcast.8, s32[1,1024]{1,0:T(1,128)} %bitcast.6, f32[1,1024]{1,0:T(1,128)} %bitcast.9, s32[1,1024]{1,0:T(1,128)} %bitcast.7, s32[15,256]{1,0:T(8,128)} %pattern_ref.1, f32[15,512,128]{2,1,0:T(8,128)} %bitcast.5), custom_call_target="tpu_custom_call" | custom-call | tf_op jit(solution)/shard_map/pallas_call | solution.py:265
  52.8 1.5 %copy.9 = f32[16,1024]{1,0:T(8,128)} copy(f32[16,1024]{1,0:T(8,128)} %shard_map.73) | data formatting | bytes 131072

commit v2 on v1

v2 whole, which is shorter than its diff:
```python
import functools

import jax
import jax.numpy as jnp
from jax import lax
from jax.experimental import pallas as pl
from jax.experimental.pallas import tpu as pltpu
from jax.sharding import PartitionSpec as P

RANK = 64
KINDS = 4
LANES = 2 * RANK
MESH = pl.DeviceIdType.MESH
F32, BF16 = jnp.float32, jnp.bfloat16
NT = (((1,), (1,)), ((), ()))
NN = (((1,), (0,)), ((), ()))


def split(x):
    hi = x.astype(BF16)
    return hi, (x - hi.astype(F32)).astype(BF16)


def dot(a, b, dims):
    return lax.dot_general(a, b, dims, preferred_element_type=F32)


def bit(x, k):
    return (x >> k) & 1


def reverse(x, n):
    return sum(bit(x, k) << (n - 1 - k) for k in range(n))


def row_of(box, level):
    if level == 7:
        return reverse(box & 127, 7)
    parts = [bit(box, level - 1 - k) << k for k in range(level)]
    parts += [bit(box, 6 + level - k) << k for k in range(level, 6)]
    return sum(parts) + (bit(box, 7) << 6)


def chebyshev(points):
    n = points.shape[1]
    x = jnp.broadcast_to(points, (8, n))
    rows = [jnp.ones_like(x), x]
    for _ in range(7):
        rows.append(2.0 * x * rows[-1] - rows[-2])
    at = lax.broadcasted_iota(jnp.int32, (8, n), 0)
    now, before = rows[0], rows[8]
    for k in range(1, 8):
        now = jnp.where(at == k, rows[k], now)
        before = jnp.where(at == k, rows[8 - k], before)
    twice = 2.0 * rows[8]
    blocks = [now]
    for _ in range(RANK // 8 - 1):
        now, before = twice * now - before, now
        blocks.append(now)
    return jnp.concatenate(blocks, axis=0)


def half_masks(basis, child):
    return jnp.concatenate([jnp.where(child == c, basis, 0.0) for c in range(2)], axis=0)


def kernel(
    V, parts, src_size, tgt_size,
    values_ref, src_offset_ref, src_box_ref, tgt_offset_ref, tgt_box_ref, pattern_ref, weights_ref,
    out_ref,
    weights, wide, kinds, work, basis_in, basis_out, sent, arrived,
    weights_sem, send_sem, recv_sem,
):
    devices = src_size * tgt_size
    levels = weights.shape[0]
    src_me, tgt_me = lax.axis_index("src"), lax.axis_index("tgt")
    me = src_me * tgt_size + tgt_me
    low, slot = lax.rem(me, 64), (me // 64) * 64
    for k in range(6):
        slot = slot + lax.rem(low // 2**k, 2) * 2 ** (5 - k)
    src_of = [lax.rem(src_me + k, src_size) for k in range(src_size)]
    tgt_of = [lax.rem(tgt_me + k, tgt_size) for k in range(tgt_size)]
    peers = [(s, t) for s in src_of for t in tgt_of][1:]

    def weights_copy(level):
        return pltpu.make_async_copy(weights_ref.at[level], weights.at[level], weights_sem.at[level])

    for level in range(levels):
        weights_copy(level).start()

    barrier = pltpu.get_barrier_semaphore()

    def greet(peer):
        pl.semaphore_signal(barrier, inc=1, device_id=peer, device_id_type=MESH)

    for peer in peers:
        greet(peer)

    def block_copy(part, peer):
        return pltpu.make_async_remote_copy(
            src_ref=sent[part].at[peer[0] * tgt_size + peer[1]],
            dst_ref=arrived[part].at[slot],
            send_sem=send_sem.at[part],
            recv_sem=recv_sem.at[part],
            device_id=peer,
            device_id_type=MESH,
        )

    lane_low = lax.broadcasted_iota(jnp.int32, (1, 1, LANES), 2) < RANK

    def set_kinds(index, level, values, order, order_rows):
        rows = lax.broadcasted_iota(jnp.int32, (128, 256), 0)
        picked = jnp.where(row_of(order, level) == rows, values, 0.0).astype(BF16)
        lane_child = (lax.broadcasted_iota(jnp.int32, (256, LANES), 1) >= RANK).astype(jnp.int32)
        spread = jnp.where(bit(order_rows, level) == lane_child, 1.0, 0.0).astype(BF16)
        kinds[index] = dot(picked, spread, NN)

    def exchange(y):
        n = y.shape[0]

        def turned(a):
            return pltpu.roll(a.reshape(n // 2 * V, LANES), RANK, 1).reshape(n // 2, V, LANES)

        top, low = y[: n // 2], y[n // 2 :]
        n0 = jnp.where(lane_low, top, turned(low))
        n1 = jnp.where(lane_low, turned(top), low)
        return jnp.stack([n0, n1], axis=1).reshape(n, V, LANES)

    def prepare(level):
        weights_copy(level).wait()
        hi, lo = split(weights[level])
        wide[level, :, :LANES] = hi
        wide[level, :, LANES : 2 * LANES] = hi
        wide[level, :, 2 * LANES :] = lo

    def product(index, x, first, n):
        hi, lo = split(x)
        all_kinds = dot(jnp.concatenate([hi, lo, hi], axis=1), wide[index], NT).reshape(n, V, KINDS * LANES)
        kind = jnp.concatenate(
            [jnp.broadcast_to(kinds[index, pl.ds(first + g, 1), :], (V, LANES))[None] for g in range(n)], axis=0
        )
        y = all_kinds[:, :, :LANES]
        for k in range(1, KINDS):
            y = jnp.where(kind == float(k), all_kinds[:, :, k * LANES : (k + 1) * LANES], y)
        return y

    def seven_levels(first, part, before, source):
        for i in range(7):
            before(i)
            halves = []
            for h in range(2):
                x = source(h) if i == 0 else work[part, h, i % 2]
                y = product(first + i, x.reshape(64 * V, LANES), 64 * h, 64)
                if i < 6:
                    work[part, h, (i + 1) % 2] = exchange(y)
                halves.append(y)
        return exchange(jnp.concatenate(halves, axis=0))

    order = lax.broadcasted_iota(jnp.int32, (1, 256), 1)
    order_rows = lax.broadcasted_iota(jnp.int32, (256, LANES), 0)

    def set_early_kinds(level):
        set_kinds(level, level, pattern_ref[level : level + 1, :].astype(F32), order, order_rows)

    set_early_kinds(0)
    rows = []
    for level in range(7, 15):
        row = pattern_ref[level : level + 1, :].astype(F32)
        rows += [row[:, :128], row[:, 128:]]
    rows = jnp.concatenate(rows + [jnp.zeros((128 - len(rows), 128), F32)], axis=0).astype(BF16)
    down = lax.broadcasted_iota(jnp.int32, (128, 128), 0)
    across = lax.broadcasted_iota(jnp.int32, (128, 128), 1)
    permute = jnp.where(reverse(down, 7) == across, 1.0, 0.0).astype(BF16)
    sent[0][:, V : V + 1, :] = dot(permute, rows, NT)[:, None, :]

    src_box = src_box_ref[...]
    src_row = row_of(src_box & 255, 0)
    hi, lo = split(half_masks(chebyshev(src_offset_ref[...]), src_box & 1))
    basis_in[:LANES] = hi
    basis_in[LANES:] = lo
    tgt_box = tgt_box_ref[...]
    tgt_row = (tgt_box >> 1) & 127
    hi, lo = split(half_masks(chebyshev(tgt_offset_ref[...]), tgt_box & 1))
    basis_out[:LANES] = hi
    basis_out[LANES : 2 * LANES] = hi
    basis_out[2 * LANES :] = lo

    def expand(part, half):
        hi, lo = split(values_ref[part * V : (part + 1) * V, :])
        here = src_row[None] == lax.broadcasted_iota(jnp.int32, (64, 1, 1), 0) + half * 64
        total = 0.0
        for term in (hi, lo):
            masked = jnp.where(here, term.astype(F32)[None], 0.0).reshape(64 * V, -1).astype(BF16)
            total += dot(masked, basis_in[...], NT)
        return total[:, :LANES] + total[:, LANES:]

    def evaluate(part, x):
        hi, lo = split(x)
        x = jnp.concatenate([hi, lo, hi], axis=1)
        n = tgt_row.shape[1]
        Q = 256
        for q in range(0, n, Q):
            h = dot(x, basis_out[:, q : q + Q], NN).reshape(128, V, Q)
            g = lax.broadcasted_iota(jnp.int32, (128, 1, 1), 0)
            total = jnp.sum(jnp.where(tgt_row[None, :, q : q + Q] == g, h, 0.0), axis=0)
            out_ref[part * V : (part + 1) * V, q : q + Q] = 0.125 * total

    def at_once(act):
        def turn(i):
            if i == 0:
                for peer in peers:
                    act(peer)

        return turn

    def nothing(i):
        pass

    def wait_all(ref, sem):
        ref = ref.at[pl.ds(0, devices - 1)]
        pltpu.make_async_copy(ref, ref, sem).wait()

    def up(part, before):
        @pl.loop(0, 1)
        def _(once):
            for h in range(2):
                work[part, h, 1] = expand(part, h).reshape(64, V, LANES)

        out = seven_levels(0, part, before, lambda h: work[part, h, 1])
        sent[part][:, :V, :] = out
        arrived[part][pl.ds(slot, 1)] = sent[part][pl.ds(me, 1)]

    prepare(0)

    def first_turn(i):
        prepare(i + 1)
        if i < 6:
            set_early_kinds(i + 1)

    up(0, first_turn)
    pl.semaphore_wait(barrier, devices - 1)
    for part in range(1, parts):
        up(part, at_once(lambda peer, part=part: block_copy(part - 1, peer).start()))

    wait_all(arrived[0], recv_sem.at[0])
    got = arrived[0][:, V, :].astype(BF16)
    pick = jnp.where(down == across, 1.0, 0.0).astype(BF16)
    got = dot(pick, got, NT)

    def source_box(place):
        at = place & 127
        return ((reverse(at & 63, 6) + (at & 64)) << 1) + (place >> 7)

    order, order_rows = source_box(order), source_box(order_rows)

    def late_row(level):
        return jnp.concatenate([got[2 * level : 2 * level + 1], got[2 * level + 1 : 2 * level + 2]], axis=1)

    def set_late_kinds(level):
        set_kinds(7 + level, level, late_row(level), order, order_rows)

    def fold_last_level():
        at_box = reverse(tgt_box & 255, 8)
        here = jnp.where(order_rows[:, :1] == at_box, 1.0, 0.0).astype(BF16)
        kind = dot(jnp.broadcast_to(late_row(7), (8, 256)).astype(BF16), here, NN)[:1]
        weights_copy(14).wait()
        turned = [jnp.transpose(weights[14, k * LANES : (k + 1) * LANES]) for k in range(KINDS)]
        hi, lo = split(jnp.concatenate(turned, axis=0))
        all_kinds = dot(jnp.concatenate([hi, lo, hi], axis=1), basis_out[...], NN)
        y = all_kinds[:LANES]
        for k in range(1, KINDS):
            y = jnp.where(kind == float(k), all_kinds[k * LANES : (k + 1) * LANES], y)
        hi, lo = split(y)
        basis_out[:LANES] = hi
        basis_out[LANES : 2 * LANES] = hi
        basis_out[2 * LANES :] = lo

    set_late_kinds(0)

    for part in range(parts):
        if part == 0:
            turn = at_once(lambda peer: block_copy(parts - 1, peer).start())

            def before(i):
                turn(i)
                if i < 6:
                    prepare(8 + i)
                    set_late_kinds(1 + i)
                if i == 3:
                    fold_last_level()
        else:
            wait_all(arrived[part], recv_sem.at[part])
            before = nothing
        x = seven_levels(7, part, before, lambda h: arrived[part][64 * h : 64 * h + 64, :V, :])
        evaluate(part, x.reshape(128 * V, LANES))

    for part in range(parts):
        wait_all(sent[part], send_sem.at[part])


def solution(mesh):
    src_size, tgt_size = mesh.shape["src"], mesh.shape["tgt"]
    devices = src_size * tgt_size
    parts = 2

    def on_device(src_values, src_offset, src_box, tgt_offset, tgt_box, pattern, operators):
        funcs, points = src_values.shape
        V = funcs // parts
        vmem = pl.BlockSpec(memory_space=pltpu.VMEM)
        blocks = [pltpu.VMEM((devices, V + (part == 0), LANES), F32) for part in range(parts)]
        return pl.pallas_call(
            functools.partial(kernel, V, parts, src_size, tgt_size),
            out_shape=jax.ShapeDtypeStruct((funcs, points), F32),
            in_specs=[vmem] * 6 + [pl.BlockSpec(memory_space=pl.ANY)],
            out_specs=vmem,
            scratch_shapes=[
                pltpu.VMEM((15, KINDS * LANES, LANES), F32),
                pltpu.VMEM((15, KINDS * LANES, 3 * LANES), BF16),
                pltpu.VMEM((15, 128, LANES), F32),
                pltpu.VMEM((parts, 2, 2, 64, V, LANES), F32),
                pltpu.VMEM((2 * LANES, points), BF16),
                pltpu.VMEM((3 * LANES, points), BF16),
                blocks,
                blocks,
                pltpu.SemaphoreType.DMA((15,)),
                pltpu.SemaphoreType.DMA((parts,)),
                pltpu.SemaphoreType.DMA((parts,)),
            ],
            compiler_params=pltpu.CompilerParams(
                collective_id=0, has_side_effects=True, vmem_limit_bytes=56 * 2**20
            ),
        )(
            src_values,
            src_offset.reshape(1, points),
            src_box.reshape(1, points),
            tgt_offset.reshape(1, points),
            tgt_box.reshape(1, points),
            pattern,
            operators.reshape(15, KINDS * LANES, LANES),
        )

    placed = (
        P(None, ("src", "tgt")),
        P(("src", "tgt")),
        P(("src", "tgt")),
        P(("src", "tgt")),
        P(("src", "tgt")),
        P(None, ("src", "tgt")),
        P(),
    )
    return jax.shard_map(
        on_device, mesh=mesh, in_specs=placed, out_specs=P(None, ("src", "tgt")), check_vma=False
    )
```

time: 54.5 us -> 44.1 us (0.81)
  Pallas kernels: 50.2 us -> 42.4 us
  other arithmetic: 2.56 us -> 0 us
    pallas_call x1, Pallas kernels: 50.2 us -> 42.4 us  [on_device(): pl.pallas_call(functools.partial(kernel, V, parts, src_size, tgt_size), o...]
    and x2 -> x0, other arithmetic: 2.56 us -> none  [the longest x1 1.28 us: on_device(): src_box.reshape(1, points) & 255]
where the time goes in v2:
time: 44.1 us; the launch traced here: 43.9 us
  Pallas kernels  42.4 us (96%)
  local copies, waits for them, and re-layouts  1.47 us (3%)
    pallas_call x1, Pallas kernels, on_device(): pl.pallas_call(functools.partial(kernel, V, parts, src_size, tgt_size), o...  42.4 us
    unnamed x1, local copies, waits for them, and re-layouts  1.47 us

profile of v2, /device:TPU:1, one launch (start us, length us, event | category | flops | bytes accessed | tf_op | source)
XLA Modules:
  0.0 43.9 jit_solution(12129634889289833473)
XLA Ops:
  0.0 42.4 %shard_map.73 = f32[16,1024]{1,0:T(8,128)} custom-call(f32[16,1024]{1,0:T(8,128)} %values_ref.1, f32[1,1024]{1,0:T(1,128)} %bitcast.6, s32[1,1024]{1,0:T(1,128)} %bitcast.7, f32[1,1024]{1,0:T(1,128)} %bitcast.8, s32[1,1024]{1,0:T(1,128)} %bitcast.9, s32[15,256]{1,0:T(8,128)} %pattern_ref.1, f32[15,512,128]{2,1,0:T(8,128)} %bitcast.5), custom_call_target="tpu_custom_call" | custom-call | tf_op jit(solution)/shard_map/pallas_call | solution.py:311
  42.4 1.5 %copy.9 = f32[16,1024]{1,0:T(8,128)} copy(f32[16,1024]{1,0:T(8,128)} %shard_map.73) | data formatting | bytes 131072

commit v3 on v2

--- a/solution.py
+++ b/solution.py
@@ -33,9 +33,14 @@
     return sum(bit(x, k) << (n - 1 - k) for k in range(n))
 
 
-def row_of(box, level):
-    if level == 7:
-        return reverse(box & 127, 7)
+def early_row(box, level, flip):
+    if level == 0:
+        return reverse(box >> 1, 7)
+    parts = [bit(box, level - 1 - k if k < level - 1 else 6 + level - k) << k for k in range(6)]
+    return sum(parts) + ((bit(box, 0) ^ flip) << 6)
+
+
+def late_row_of(box, level):
     parts = [bit(box, level - 1 - k) << k for k in range(level)]
     parts += [bit(box, 6 + level - k) << k for k in range(level, 6)]
     return sum(parts) + (bit(box, 7) << 6)
@@ -65,10 +70,10 @@
 
 
 def kernel(
-    V, parts, src_size, tgt_size,
+    V, parts, lag, src_size, tgt_size,
     values_ref, src_offset_ref, src_box_ref, tgt_offset_ref, tgt_box_ref, pattern_ref, weights_ref,
     out_ref,
-    weights, wide, kinds, work, basis_in, basis_out, sent, arrived,
+    weights, wide, last, kinds, work, basis_in, basis_out, sent, arrived,
     weights_sem, send_sem, recv_sem,
 ):
     devices = src_size * tgt_size
@@ -81,6 +86,14 @@
     src_of = [lax.rem(src_me + k, src_size) for k in range(src_size)]
     tgt_of = [lax.rem(tgt_me + k, tgt_size) for k in range(tgt_size)]
     peers = [(s, t) for s in src_of for t in tgt_of][1:]
+    group = src_size // 2
+    my_half = src_me // group
+    flip = 1 - my_half
+    in_half = [lax.rem(src_me + k, group) for k in range(group)]
+    groups = [
+        [(flip * group + s, t) for s in in_half for t in tgt_of],
+        [(my_half * group + s, t) for s in in_half for t in tgt_of][1:],
+    ]
 
     def weights_copy(level):
         return pltpu.make_async_copy(weights_ref.at[level], weights.at[level], weights_sem.at[level])
@@ -96,9 +109,10 @@
     for peer in peers:
         greet(peer)
 
-    def block_copy(part, peer):
+    def block_copy(part, which, peer):
+        row = which * 64 + lax.rem(peer[0], group) * tgt_size + peer[1]
         return pltpu.make_async_remote_copy(
-            src_ref=sent[part].at[peer[0] * tgt_size + peer[1]],
+            src_ref=sent[part].at[row],
             dst_ref=arrived[part].at[slot],
             send_sem=send_sem.at[part],
             recv_sem=recv_sem.at[part],
@@ -108,14 +122,14 @@
 
     lane_low = lax.broadcasted_iota(jnp.int32, (1, 1, LANES), 2) < RANK
 
-    def set_kinds(index, level, values, order, order_rows):
+    def set_kinds(index, level, values, row_in_order, order_rows):
         rows = lax.broadcasted_iota(jnp.int32, (128, 256), 0)
-        picked = jnp.where(row_of(order, level) == rows, values, 0.0).astype(BF16)
+        picked = jnp.where(row_in_order == rows, values, 0.0).astype(BF16)
         lane_child = (lax.broadcasted_iota(jnp.int32, (256, LANES), 1) >= RANK).astype(jnp.int32)
         spread = jnp.where(bit(order_rows, level) == lane_child, 1.0, 0.0).astype(BF16)
         kinds[index] = dot(picked, spread, NN)
 
-    def exchange(y):
+    def swap(y):
         n = y.shape[0]
 
         def turned(a):
@@ -124,7 +138,10 @@
         top, low = y[: n // 2], y[n // 2 :]
         n0 = jnp.where(lane_low, top, turned(low))
         n1 = jnp.where(lane_low, turned(top), low)
-        return jnp.stack([n0, n1], axis=1).reshape(n, V, LANES)
+        return n0, n1
+
+    def exchange(y):
+        return jnp.stack(swap(y), axis=1).reshape(y.shape[0], V, LANES)
 
     def prepare(level):
         weights_copy(level).wait()
@@ -144,46 +161,53 @@
             y = jnp.where(kind == float(k), all_kinds[:, :, k * LANES : (k + 1) * LANES], y)
         return y
 
-    def seven_levels(first, part, before, source):
-        for i in range(7):
+    def on_halves(levels_here, part, before, source):
+        for i, index in enumerate(levels_here):
             before(i)
             halves = []
             for h in range(2):
-                x = source(h) if i == 0 else work[part, h, i % 2]
-                y = product(first + i, x.reshape(64 * V, LANES), 64 * h, 64)
-                if i < 6:
+                y = source(h) if i == 0 else work[part, h, i % 2]
+                if index is not None:
+                    y = product(index, y.reshape(64 * V, LANES), 64 * h, 64)
+                if i < len(levels_here) - 1:
                     work[part, h, (i + 1) % 2] = exchange(y)
                 halves.append(y)
         return exchange(jnp.concatenate(halves, axis=0))
 
     order = lax.broadcasted_iota(jnp.int32, (1, 256), 1)
     order_rows = lax.broadcasted_iota(jnp.int32, (256, LANES), 0)
-
-    def set_early_kinds(level):
-        set_kinds(level, level, pattern_ref[level : level + 1, :].astype(F32), order, order_rows)
-
-    set_early_kinds(0)
-    rows = []
-    for level in range(7, 15):
-        row = pattern_ref[level : level + 1, :].astype(F32)
-        rows += [row[:, :128], row[:, 128:]]
-    rows = jnp.concatenate(rows + [jnp.zeros((128 - len(rows), 128), F32)], axis=0).astype(BF16)
     down = lax.broadcasted_iota(jnp.int32, (128, 128), 0)
     across = lax.broadcasted_iota(jnp.int32, (128, 128), 1)
-    permute = jnp.where(reverse(down, 7) == across, 1.0, 0.0).astype(BF16)
-    sent[0][:, V : V + 1, :] = dot(permute, rows, NT)[:, None, :]
+
+    def set_early_kinds(level):
+        values = pattern_ref[level : level + 1, :].astype(F32)
+        set_kinds(level, level, values, early_row(order, level, flip), order_rows)
+
+    def set_pattern_row():
+        rows = []
+        for level in range(7, 15):
+            row = pattern_ref[level : level + 1, :].astype(F32)
+            rows += [row[:, :128], row[:, 128:]]
+        rows = jnp.concatenate(rows + [jnp.zeros((128 - len(rows), 128), F32)], axis=0).astype(BF16)
+        permute = jnp.where(reverse(down ^ (flip << 6), 7) == across, 1.0, 0.0).astype(BF16)
+        sent[0][:, V : V + 1, :] = dot(permute, rows, NT)[:, None, :]
 
     src_box = src_box_ref[...]
-    src_row = row_of(src_box & 255, 0)
+    src_row = early_row(src_box & 255, 0, flip)
     hi, lo = split(half_masks(chebyshev(src_offset_ref[...]), src_box & 1))
     basis_in[:LANES] = hi
     basis_in[LANES:] = lo
     tgt_box = tgt_box_ref[...]
     tgt_row = (tgt_box >> 1) & 127
-    hi, lo = split(half_masks(chebyshev(tgt_offset_ref[...]), tgt_box & 1))
-    basis_out[:LANES] = hi
-    basis_out[LANES : 2 * LANES] = hi
-    basis_out[2 * LANES :] = lo
+
+    def set_basis_out(z):
+        hi, lo = split(z)
+        basis_out[:LANES] = hi
+        basis_out[LANES : 2 * LANES] = hi
+        basis_out[2 * LANES :] = lo
+
+    def target_basis():
+        set_basis_out(half_masks(chebyshev(tgt_offset_ref[...]), tgt_box & 1))
 
     def expand(part, half):
         hi, lo = split(values_ref[part * V : (part + 1) * V, :])
@@ -205,14 +229,6 @@
             total = jnp.sum(jnp.where(tgt_row[None, :, q : q + Q] == g, h, 0.0), axis=0)
             out_ref[part * V : (part + 1) * V, q : q + Q] = 0.125 * total
 
-    def at_once(act):
-        def turn(i):
-            if i == 0:
-                for peer in peers:
-                    act(peer)
-
-        return turn
-
     def nothing(i):
         pass
 
@@ -226,21 +242,69 @@
             for h in range(2):
                 work[part, h, 1] = expand(part, h).reshape(64, V, LANES)
 
-        out = seven_levels(0, part, before, lambda h: work[part, h, 1])
-        sent[part][:, :V, :] = out
-        arrived[part][pl.ds(slot, 1)] = sent[part][pl.ds(me, 1)]
-
+        before(0)
+        y = [product(0, work[part, h, 1].reshape(64 * V, LANES), 64 * h, 64) for h in range(2)]
+        zero, one = swap(jnp.concatenate(y, axis=0))
+        work[part, 0, 0] = jnp.where(flip == 1, one, zero)
+        work[part, 1, 0] = jnp.where(flip == 1, zero, one)
+        for step in range(1, 8 + lag):
+            before(step)
+            for which in range(2):
+                level = step - lag * which
+                if not 1 <= level <= 7:
+                    continue
+                y = product(level, work[part, which, (level - 1) % 2].reshape(64 * V, LANES), 64 * which, 64)
+                if level < 7:
+                    work[part, which, level % 2] = exchange(y)
+                else:
+                    sent[part][64 * which : 64 * which + 64, :V, :] = y
+
+        arrived[part][pl.ds(slot, 1)] = sent[part][pl.ds(64 + lax.rem(me, 64), 1)]
+
+    def send(part, which):
+        for peer in groups[which]:
+            block_copy(part, which, peer).start()
+
+    def apply_last_weights():
+        weights_copy(14).wait()
+        turned = [jnp.transpose(weights[14, k * LANES : (k + 1) * LANES]) for k in range(KINDS)]
+        hi, lo = split(jnp.concatenate(turned, axis=0))
+        last[...] = dot(jnp.concatenate([hi, lo, hi], axis=1), basis_out[...], NN)
+
+    set_early_kinds(0)
     prepare(0)
 
-    def first_turn(i):
-        prepare(i + 1)
-        if i < 6:
+    def beside_first(i):
+        if i < 7:
+            prepare(i + 1)
             set_early_kinds(i + 1)
-
-    up(0, first_turn)
-    pl.semaphore_wait(barrier, devices - 1)
-    for part in range(1, parts):
-        up(part, at_once(lambda peer, part=part: block_copy(part - 1, peer).start()))
+        if i == 2:
+            set_pattern_row()
+        if i == 8:
+            pl.semaphore_wait(barrier, devices - 1)
+            send(0, 0)
+
+    up(0, beside_first)
+    if lag == 0:
+        pl.semaphore_wait(barrier, devices - 1)
+        send(0, 0)
+
+    def beside_second(i):
+        if i == 0:
+            send(0, 1)
+        elif i < 7:
+            prepare(7 + i)
+        if i == 1:
+            target_basis()
+        if i == 4:
+            apply_last_weights()
+        if i == 8:
+            send(1, 0)
+
+    up(1, beside_second)
+    if lag == 0:
+        send(1, 0)
+    send(1, 1)
 
     wait_all(arrived[0], recv_sem.at[0])
     got = arrived[0][:, V, :].astype(BF16)
@@ -251,47 +315,38 @@
         at = place & 127
         return ((reverse(at & 63, 6) + (at & 64)) << 1) + (place >> 7)
 
-    order, order_rows = source_box(order), source_box(order_rows)
+    late_order, late_order_rows = source_box(order), source_box(order_rows)
 
     def late_row(level):
         return jnp.concatenate([got[2 * level : 2 * level + 1], got[2 * level + 1 : 2 * level + 2]], axis=1)
 
     def set_late_kinds(level):
-        set_kinds(7 + level, level, late_row(level), order, order_rows)
-
-    def fold_last_level():
+        set_kinds(7 + level, level, late_row(level), late_row_of(late_order, level), late_order_rows)
+
+    def pick_last_kind():
         at_box = reverse(tgt_box & 255, 8)
-        here = jnp.where(order_rows[:, :1] == at_box, 1.0, 0.0).astype(BF16)
+        here = jnp.where(late_order_rows[:, :1] == at_box, 1.0, 0.0).astype(BF16)
         kind = dot(jnp.broadcast_to(late_row(7), (8, 256)).astype(BF16), here, NN)[:1]
-        weights_copy(14).wait()
-        turned = [jnp.transpose(weights[14, k * LANES : (k + 1) * LANES]) for k in range(KINDS)]
-        hi, lo = split(jnp.concatenate(turned, axis=0))
-        all_kinds = dot(jnp.concatenate([hi, lo, hi], axis=1), basis_out[...], NN)
-        y = all_kinds[:LANES]
+        z = last[:LANES]
         for k in range(1, KINDS):
-            y = jnp.where(kind == float(k), all_kinds[k * LANES : (k + 1) * LANES], y)
-        hi, lo = split(y)
-        basis_out[:LANES] = hi
-        basis_out[LANES : 2 * LANES] = hi
-        basis_out[2 * LANES :] = lo
-
-    set_late_kinds(0)
+            z = jnp.where(kind == float(k), last[k * LANES : (k + 1) * LANES], z)
+        set_basis_out(z)
+
+    def beside_third(i):
+        if i < 6:
+            set_late_kinds(1 + i)
+        if i == 4:
+            pick_last_kind()
 
     for part in range(parts):
-        if part == 0:
-            turn = at_once(lambda peer: block_copy(parts - 1, peer).start())
-
-            def before(i):
-                turn(i)
-                if i < 6:
-                    prepare(8 + i)
-                    set_late_kinds(1 + i)
-                if i == 3:
-                    fold_last_level()
-        else:
+        if part > 0:
             wait_all(arrived[part], recv_sem.at[part])
-            before = nothing
-        x = seven_levels(7, part, before, lambda h: arrived[part][64 * h : 64 * h + 64, :V, :])
+        x = on_halves(
+            [None] + list(range(8, 14)),
+            part,
+            nothing if part else beside_third,
+            lambda h: arrived[part][64 * h : 64 * h + 64, :V, :],
+        )
         evaluate(part, x.reshape(128 * V, LANES))
 
     for part in range(parts):
@@ -301,7 +356,7 @@
 def solution(mesh):
     src_size, tgt_size = mesh.shape["src"], mesh.shape["tgt"]
     devices = src_size * tgt_size
-    parts = 2
+    parts, lag = 2, 3
 
     def on_device(src_values, src_offset, src_box, tgt_offset, tgt_box, pattern, operators):
         funcs, points = src_values.shape
@@ -309,13 +364,14 @@
         vmem = pl.BlockSpec(memory_space=pltpu.VMEM)
         blocks = [pltpu.VMEM((devices, V + (part == 0), LANES), F32) for part in range(parts)]
         return pl.pallas_call(
-            functools.partial(kernel, V, parts, src_size, tgt_size),
+            functools.partial(kernel, V, parts, lag, src_size, tgt_size),
             out_shape=jax.ShapeDtypeStruct((funcs, points), F32),
             in_specs=[vmem] * 6 + [pl.BlockSpec(memory_space=pl.ANY)],
             out_specs=vmem,
             scratch_shapes=[
                 pltpu.VMEM((15, KINDS * LANES, LANES), F32),
                 pltpu.VMEM((15, KINDS * LANES, 3 * LANES), BF16),
+                pltpu.VMEM((KINDS * LANES, points), F32),
                 pltpu.VMEM((15, 128, LANES), F32),
                 pltpu.VMEM((parts, 2, 2, 64, V, LANES), F32),
                 pltpu.VMEM((2 * LANES, points), BF16),

time: 44.1 us -> 41.8 us (0.948)
  Pallas kernels: 42.4 us -> 40.1 us
    pallas_call x1, Pallas kernels: 42.4 us -> 40.1 us  [on_device(): pl.pallas_call(functools.partial(kernel, V, parts, lag, src_size, tgt_siz...]
where the time goes in v3:
time: 41.8 us; the launch traced here: 41.6 us
  Pallas kernels  40.1 us (96%)
  local copies, waits for them, and re-layouts  1.47 us (4%)
    pallas_call x1, Pallas kernels, on_device(): pl.pallas_call(functools.partial(kernel, V, parts, lag, src_size, tgt_siz...  40.1 us
    unnamed x1, local copies, waits for them, and re-layouts  1.47 us

profile of v3, /device:TPU:1, one launch (start us, length us, event | category | flops | bytes accessed | tf_op | source)
XLA Modules:
  0.0 41.6 jit_solution(7511201497356733335)
XLA Ops:
  0.0 40.1 %shard_map.73 = f32[16,1024]{1,0:T(8,128)} custom-call(f32[16,1024]{1,0:T(8,128)} %values_ref.1, f32[1,1024]{1,0:T(1,128)} %bitcast.6, s32[1,1024]{1,0:T(1,128)} %bitcast.7, f32[1,1024]{1,0:T(1,128)} %bitcast.8, s32[1,1024]{1,0:T(1,128)} %bitcast.9, s32[15,256]{1,0:T(8,128)} %pattern_ref.1, f32[15,512,128]{2,1,0:T(8,128)} %bitcast.5), custom_call_target="tpu_custom_call" | custom-call | tf_op jit(solution)/shard_map/pallas_call | solution.py:366
  40.1 1.5 %copy.9 = f32[16,1024]{1,0:T(8,128)} copy(f32[16,1024]{1,0:T(8,128)} %shard_map.73) | data formatting | bytes 131072

commit v4 on v3

--- a/solution.py
+++ b/solution.py
@@ -292,12 +292,6 @@
     def beside_second(i):
         if i == 0:
             send(0, 1)
-        elif i < 7:
-            prepare(7 + i)
-        if i == 1:
-            target_basis()
-        if i == 4:
-            apply_last_weights()
         if i == 8:
             send(1, 0)
 
@@ -305,6 +299,10 @@
     if lag == 0:
         send(1, 0)
     send(1, 1)
+    target_basis()
+    apply_last_weights()
+    for level in range(8, 14):
+        prepare(level)
 
     wait_all(arrived[0], recv_sem.at[0])
     got = arrived[0][:, V, :].astype(BF16)

time: 41.8 us -> 39.7 us (0.950)
  Pallas kernels: 40.1 us -> 38 us
    pallas_call x1, Pallas kernels: 40.1 us -> 38 us  [on_device(): pl.pallas_call(functools.partial(kernel, V, parts, lag, src_size, tgt_siz...]
where the time goes in v4:
time: 39.7 us; the launch traced here: 39.5 us
  Pallas kernels  38 us (96%)
  local copies, waits for them, and re-layouts  1.47 us (4%)
    pallas_call x1, Pallas kernels, on_device(): pl.pallas_call(functools.partial(kernel, V, parts, lag, src_size, tgt_siz...  38 us
    unnamed x1, local copies, waits for them, and re-layouts  1.47 us

profile of v4, /device:TPU:1, one launch (start us, length us, event | category | flops | bytes accessed | tf_op | source)
XLA Modules:
  0.0 39.5 jit_solution(9576632857241556915)
XLA Ops:
  0.0 38.0 %shard_map.73 = f32[16,1024]{1,0:T(8,128)} custom-call(f32[16,1024]{1,0:T(8,128)} %values_ref.1, f32[1,1024]{1,0:T(1,128)} %bitcast.6, s32[1,1024]{1,0:T(1,128)} %bitcast.7, f32[1,1024]{1,0:T(1,128)} %bitcast.8, s32[1,1024]{1,0:T(1,128)} %bitcast.9, s32[15,256]{1,0:T(8,128)} %pattern_ref.1, f32[15,512,128]{2,1,0:T(8,128)} %bitcast.5), custom_call_target="tpu_custom_call" | custom-call | tf_op jit(solution)/shard_map/pallas_call | solution.py:364
  38.0 1.5 %copy.9 = f32[16,1024]{1,0:T(8,128)} copy(f32[16,1024]{1,0:T(8,128)} %shard_map.73) | data formatting | bytes 131072

commit v5 on v4

--- a/solution.py
+++ b/solution.py
@@ -222,7 +222,7 @@
         hi, lo = split(x)
         x = jnp.concatenate([hi, lo, hi], axis=1)
         n = tgt_row.shape[1]
-        Q = 256
+        Q = 512
         for q in range(0, n, Q):
             h = dot(x, basis_out[:, q : q + Q], NN).reshape(128, V, Q)
             g = lax.broadcasted_iota(jnp.int32, (128, 1, 1), 0)
@@ -237,10 +237,8 @@
         pltpu.make_async_copy(ref, ref, sem).wait()
 
     def up(part, before):
-        @pl.loop(0, 1)
-        def _(once):
-            for h in range(2):
-                work[part, h, 1] = expand(part, h).reshape(64, V, LANES)
+        for h in range(2):
+            work[part, h, 1] = expand(part, h).reshape(64, V, LANES)
 
         before(0)
         y = [product(0, work[part, h, 1].reshape(64 * V, LANES), 64 * h, 64) for h in range(2)]

time: 39.7 us -> 39.7 us (level)
  no operation moved by 1% of the time
where the time goes in v5:
time: 39.7 us; the launch traced here: 39.5 us
  Pallas kernels  38 us (96%)
  local copies, waits for them, and re-layouts  1.47 us (4%)
    pallas_call x1, Pallas kernels, on_device(): pl.pallas_call(functools.partial(kernel, V, parts, lag, src_size, tgt_siz...  38 us
    unnamed x1, local copies, waits for them, and re-layouts  1.47 us

profile of v5, /device:TPU:1, one launch (start us, length us, event | category | flops | bytes accessed | tf_op | source)
XLA Modules:
  0.0 39.5 jit_solution(18338937014230098380)
XLA Ops:
  0.0 38.0 %shard_map.73 = f32[16,1024]{1,0:T(8,128)} custom-call(f32[16,1024]{1,0:T(8,128)} %values_ref.1, f32[1,1024]{1,0:T(1,128)} %bitcast.6, s32[1,1024]{1,0:T(1,128)} %bitcast.7, f32[1,1024]{1,0:T(1,128)} %bitcast.8, s32[1,1024]{1,0:T(1,128)} %bitcast.9, s32[15,256]{1,0:T(8,128)} %pattern_ref.1, f32[15,512,128]{2,1,0:T(8,128)} %bitcast.5), custom_call_target="tpu_custom_call" | custom-call | tf_op jit(solution)/shard_map/pallas_call | solution.py:362
  38.0 1.5 %copy.9 = f32[16,1024]{1,0:T(8,128)} copy(f32[16,1024]{1,0:T(8,128)} %shard_map.73) | data formatting | bytes 131072
